TPU v7x, 32 devices: a whole 2x2x4 slice. The times are simulated.
32 devices in a mesh: dp: 4 (over z), row: 4 (over y, core), col: 2 (over x).
Axes of the slice: x: 2, y: 2, z: 4, core: 2. Of those that a mesh axis runs over, the one named last changes fastest.
Arguments:
- tokens: bfloat16 [12288, 768], P(('dp', 'row'), 'col'), may hold values from -6 to 6
- query_weight: bfloat16 [768, 768], P('col', 'row'), may hold values from -0.21875 to 0.21875
- key_weight: bfloat16 [768, 768], P('col', 'row'), may hold values from -0.21875 to 0.21875
- value_weight: bfloat16 [768, 768], P('col', 'row'), may hold values from -0.21875 to 0.21875
- query_bias: float32 [768], P('row'), may hold values from -3 to 3
- value_bias: float32 [768], P('row'), may hold values from -3 to 3
- out_weight: bfloat16 [768, 768], P('row', 'col'), may hold values from -3 to 3
- out_bias: float32 [768], P('col'), may hold values from -3 to 3
- up_weight: bfloat16 [768, 3072], P('col', 'row'), may hold values from -0.21875 to 0.21875
- up_bias: float32 [3072], P('row'), may hold values from -3 to 3
- down_weight: bfloat16 [3072, 768], P('row', 'col'), may hold values from -0.109375 to 0.109375
- down_bias: float32 [768], P('col'), may hold values from -3 to 3
- attn_gain: float32 [768], P('col'), may hold values from 0.5 to 2
- attn_shift: float32 [768], P('col'), may hold values from -3 to 3
- mlp_gain: float32 [768], P('col'), may hold values from 0.5 to 2
- mlp_shift: float32 [768], P('col'), may hold values from -3 to 3
- cotangent: bfloat16 [12288, 768], P(('dp', 'row'), 'col'), may hold values from -6 to 6
Outputs:
- outputs: bfloat16 [12288, 768], P(('dp', 'row'), 'col')
- input_grad: float32 [12288, 768], P(('dp', 'row'), 'col')
- query_weight_grad: float32 [768, 768], P(('col', 'dp'), 'row')
- key_weight_grad: float32 [768, 768], P(('col', 'dp'), 'row')
- value_weight_grad: float32 [768, 768], P(('col', 'dp'), 'row')
- query_bias_grad: float32 [768], P(('row', 'dp'))
- value_bias_grad: float32 [768], P(('row', 'dp'))
- out_weight_grad: float32 [768, 768], P('row', ('col', 'dp'))
- out_bias_grad: float32 [768], P(('col', 'dp'))
- up_weight_grad: float32 [768, 3072], P(('col', 'dp'), 'row')
- up_bias_grad: float32 [3072], P(('row', 'dp'))
- down_weight_grad: float32 [3072, 768], P('row', ('col', 'dp'))
- down_bias_grad: float32 [768], P(('col', 'dp'))
- attn_gain_grad: float32 [768], P(('col', 'dp'))
- attn_shift_grad: float32 [768], P(('col', 'dp'))
- mlp_gain_grad: float32 [768], P(('col', 'dp'))
- mlp_shift_grad: float32 [768], P(('col', 'dp'))
All inputs are finite; a program needn't handle non-finite values.
Results may differ from a plain program's by a relative error of at most 0.012.
The roundings to bfloat16 on the way count: a program that leaves them out, or rounds other values in their place, can miss the bound.
Values may be sent and summed in bfloat16 or wider, within the bound.
No kernel may reach another device: no remote copies, remote signals or barrier semaphores. Data moves between devices by JAX's collectives and lax.ppermute only.
A program may use at most 128 MiB of HBM per device.

v0:
```python
import jax
import jax.numpy as jnp
from jax import lax
from jax.sharding import PartitionSpec as P

HD = 64
QBLK = 512


epsilon = 1e-05


def token_sums(first, second):
    return lax.psum((first, second), "col")


def normalize(values, gain, shift):
    width = values.shape[1] * lax.axis_size("col")
    totals, squares = token_sums(jnp.sum(values, axis=1), jnp.sum(values * values, axis=1))
    center = totals / width
    inverse = lax.rsqrt(squares / width - center * center + epsilon)
    normed = (values - center[:, None]) * inverse[:, None]
    return ((normed * gain + shift).astype(jnp.bfloat16), normed, inverse)


def normalize_back(upstream, normed, inverse, gain):
    width = normed.shape[1] * lax.axis_size("col")
    scaled = upstream * gain
    first, second = token_sums(jnp.sum(scaled, axis=1), jnp.sum(scaled * normed, axis=1))
    return inverse[:, None] * (scaled - first[:, None] / width - normed * second[:, None] / width)


def project_up(normed_rows, weight_block):
    gathered = lax.all_gather(normed_rows, "row", axis=0, tiled=True)
    pieces = jnp.dot(gathered, weight_block, preferred_element_type=jnp.float32)
    result = lax.psum_scatter(pieces, "col", scatter_dimension=0, tiled=True)
    return (gathered, result)


def up_back(grad_rows, kept_rows, weight_block):
    gathered = lax.all_gather(grad_rows, "col", axis=0, tiled=True)
    weight_grad = jnp.dot(kept_rows.T, gathered, preferred_element_type=jnp.float32)
    bias_grad = jnp.sum(gathered.astype(jnp.float32), axis=0)
    pieces = jnp.dot(gathered, weight_block.T, preferred_element_type=jnp.float32)
    return (
        weight_grad,
        bias_grad,
        lax.psum_scatter(pieces, "row", scatter_dimension=0, tiled=True),
    )


def project_down(values, weight_block):
    gathered = lax.all_gather(values, "col", axis=0, tiled=True)
    pieces = jnp.dot(gathered, weight_block, preferred_element_type=jnp.float32)
    return (gathered, lax.psum_scatter(pieces, "row", scatter_dimension=0, tiled=True))


def down_back(grad_rows, kept_rows, weight_block):
    gathered = lax.all_gather(grad_rows, "row", axis=0, tiled=True)
    weight_grad = jnp.dot(kept_rows.T, gathered, preferred_element_type=jnp.float32)
    bias_grad = jnp.sum(gathered.astype(jnp.float32), axis=0)
    pieces = jnp.dot(gathered, weight_block.T, preferred_element_type=jnp.float32)
    result = lax.psum_scatter(pieces, "col", scatter_dimension=0, tiled=True)
    return (weight_grad, bias_grad, result)


def masked_scores(query_block, key_heads, start):
    block_rows = query_block.shape[0]
    length = key_heads.shape[0]
    scores = jnp.einsum(
        "qhd,khd->hqk", query_block, key_heads, preferred_element_type=jnp.float32
    ) * HD ** (-0.5)
    row_ids = start + lax.broadcasted_iota(jnp.int32, (block_rows, length), 0)
    col_ids = lax.broadcasted_iota(jnp.int32, (block_rows, length), 1)
    return jnp.where((col_ids <= row_ids)[None], scores, -1e30)


def attend(queries, key_rows, value_rows):
    length, features = queries.shape
    block_rows = min(QBLK, length)
    query_heads = queries.reshape(length, features // HD, HD)
    key_heads = key_rows.reshape(length, features // HD, HD)
    value_heads = value_rows.reshape(length, features // HD, HD)

    def forward_block(start):
        query_block = lax.dynamic_slice_in_dim(query_heads, start, block_rows, 0)
        scores = masked_scores(query_block, key_heads, start)
        top = jnp.max(scores, axis=-1, keepdims=True)
        powers = jnp.exp(scores - top)
        total = jnp.sum(powers, axis=-1, keepdims=True)
        probs = (powers / total).astype(jnp.bfloat16)
        output = jnp.einsum("hqk,khd->qhd", probs, value_heads, preferred_element_type=jnp.float32)
        return (output.astype(jnp.bfloat16), top[..., 0] + jnp.log(total[..., 0]))

    starts = jnp.arange(length // block_rows) * block_rows
    outputs, logsum = lax.map(forward_block, starts)
    return (outputs.reshape(length, features), logsum)


def attend_back(queries, key_rows, value_rows, logsum, grad_out):
    length, features = queries.shape
    block_rows = min(QBLK, length)
    score_scale = HD ** (-0.5)
    query_heads = queries.reshape(length, features // HD, HD)
    key_heads = key_rows.reshape(length, features // HD, HD)
    value_heads = value_rows.reshape(length, features // HD, HD)
    grad_heads = grad_out.reshape(length, features // HD, HD)

    def backward_block(carry, item):
        key_grad, value_grad = carry
        start, block_logsum = item
        query_block = lax.dynamic_slice_in_dim(query_heads, start, block_rows, 0)
        grad_block = lax.dynamic_slice_in_dim(grad_heads, start, block_rows, 0)
        scores = masked_scores(query_block, key_heads, start)
        probs = jnp.exp(scores - block_logsum[..., None])
        value_grad = value_grad + jnp.einsum(
            "hqk,qhd->khd",
            probs.astype(jnp.bfloat16),
            grad_block,
            preferred_element_type=jnp.float32,
        )
        prob_grad = jnp.einsum(
            "qhd,khd->hqk", grad_block, value_heads, preferred_element_type=jnp.float32
        )
        row_dot = jnp.sum(prob_grad * probs, axis=-1, keepdims=True)
        score_grad = (probs * (prob_grad - row_dot)).astype(jnp.bfloat16)
        query_grad = (
            jnp.einsum("hqk,khd->qhd", score_grad, key_heads, preferred_element_type=jnp.float32)
            * score_scale
        )
        key_grad = (
            key_grad
            + jnp.einsum(
                "hqk,qhd->khd", score_grad, query_block, preferred_element_type=jnp.float32
            )
            * score_scale
        )
        return ((key_grad, value_grad), query_grad)

    starts = jnp.arange(length // block_rows) * block_rows
    zeros = jnp.zeros((length, features // HD, HD), jnp.float32)
    (key_grad, value_grad), query_grad = lax.scan(backward_block, (zeros, zeros), (starts, logsum))
    return (
        query_grad.reshape(length, features),
        key_grad.reshape(length, features),
        value_grad.reshape(length, features),
    )


def gelu_tanh(values):
    return jax.nn.gelu(values, approximate=True)


def local(
    tokens,
    query_weight,
    key_weight,
    value_weight,
    query_bias,
    value_bias,
    out_weight,
    out_bias,
    up_weight,
    up_bias,
    down_weight,
    down_bias,
    attn_gain,
    attn_shift,
    mlp_gain,
    mlp_shift,
    cotangent,
):
    inputs = tokens.astype(jnp.float32)
    first_in, first_norm, first_inv = normalize(inputs, attn_gain, attn_shift)
    qkv_weight = jnp.concatenate((query_weight, key_weight, value_weight), axis=1)
    first_gathered, qkv_sum = project_up(first_in, qkv_weight)
    quarter = query_weight.shape[1]
    queries = (qkv_sum[:, :quarter] + query_bias).astype(jnp.bfloat16)
    key_rows = qkv_sum[:, quarter : 2 * quarter].astype(jnp.bfloat16)
    value_rows = (qkv_sum[:, 2 * quarter :] + value_bias).astype(jnp.bfloat16)
    attended, logsum = attend(queries, key_rows, value_rows)
    attn_gathered, attn_sum = project_down(attended, out_weight)
    middle = inputs + (attn_sum + out_bias)
    second_in, second_norm, second_inv = normalize(middle, mlp_gain, mlp_shift)
    second_gathered, hidden_sum = project_up(second_in, up_weight)
    hidden_pre = hidden_sum + up_bias
    hidden = gelu_tanh(hidden_pre).astype(jnp.bfloat16)
    hidden_gathered, mlp_sum = project_down(hidden, down_weight)
    outputs = (middle + (mlp_sum + down_bias)).astype(jnp.bfloat16)
    upstream = cotangent.astype(jnp.float32)
    down_w_grad, down_b_grad, hidden_grad = down_back(cotangent, hidden_gathered, down_weight)
    gelu_grad = jax.vjp(gelu_tanh, hidden_pre)[1](hidden_grad)[0]
    up_w_grad, up_b_grad, second_grad = up_back(
        gelu_grad.astype(jnp.bfloat16), second_gathered, up_weight
    )
    mlp_gain_part = jnp.sum(second_grad * second_norm, axis=0)
    mlp_shift_part = jnp.sum(second_grad, axis=0)
    middle_grad = upstream + normalize_back(second_grad, second_norm, second_inv, mlp_gain)
    out_w_grad, out_b_grad, attended_grad = down_back(
        middle_grad.astype(jnp.bfloat16), attn_gathered, out_weight
    )
    query_grad, key_grad, value_grad = attend_back(
        queries, key_rows, value_rows, logsum, attended_grad.astype(jnp.bfloat16)
    )
    qkv_grad = jnp.concatenate((query_grad, key_grad, value_grad), axis=1).astype(jnp.bfloat16)
    qkv_w_grad, qkv_b_grad, first_grad = up_back(qkv_grad, first_gathered, qkv_weight)
    attn_gain_part = jnp.sum(first_grad * first_norm, axis=0)
    attn_shift_part = jnp.sum(first_grad, axis=0)
    input_grad = middle_grad + normalize_back(first_grad, first_norm, first_inv, attn_gain)
    attn_gain_sum, attn_shift_sum, mlp_gain_sum, mlp_shift_sum = lax.psum(
        (attn_gain_part, attn_shift_part, mlp_gain_part, mlp_shift_part), "row"
    )
    reduced = (
        lax.psum_scatter(qkv_w_grad[:, :quarter], "dp", scatter_dimension=0, tiled=True),
        lax.psum_scatter(
            qkv_w_grad[:, quarter : 2 * quarter], "dp", scatter_dimension=0, tiled=True
        ),
        lax.psum_scatter(qkv_w_grad[:, 2 * quarter :], "dp", scatter_dimension=0, tiled=True),
        lax.psum_scatter(qkv_b_grad[:quarter], "dp", scatter_dimension=0, tiled=True),
        lax.psum_scatter(qkv_b_grad[2 * quarter :], "dp", scatter_dimension=0, tiled=True),
        lax.psum_scatter(out_w_grad, "dp", scatter_dimension=1, tiled=True),
        lax.psum_scatter(out_b_grad, "dp", scatter_dimension=0, tiled=True),
        lax.psum_scatter(up_w_grad, "dp", scatter_dimension=0, tiled=True),
        lax.psum_scatter(up_b_grad, "dp", scatter_dimension=0, tiled=True),
        lax.psum_scatter(down_w_grad, "dp", scatter_dimension=1, tiled=True),
        lax.psum_scatter(down_b_grad, "dp", scatter_dimension=0, tiled=True),
        lax.psum_scatter(attn_gain_sum, "dp", scatter_dimension=0, tiled=True),
        lax.psum_scatter(attn_shift_sum, "dp", scatter_dimension=0, tiled=True),
        lax.psum_scatter(mlp_gain_sum, "dp", scatter_dimension=0, tiled=True),
        lax.psum_scatter(mlp_shift_sum, "dp", scatter_dimension=0, tiled=True),
    )
    return (
        outputs,
        input_grad,
        reduced[0],
        reduced[1],
        reduced[2],
        reduced[3],
        reduced[4],
        reduced[5],
        reduced[6],
        reduced[7],
        reduced[8],
        reduced[9],
        reduced[10],
        reduced[11],
        reduced[12],
        reduced[13],
        reduced[14],
    )


def solution(mesh):
    placed = (
        P(("dp", "row"), "col"),
        P("col", "row"),
        P("col", "row"),
        P("col", "row"),
        P("row"),
        P("row"),
        P("row", "col"),
        P("col"),
        P("col", "row"),
        P("row"),
        P("row", "col"),
        P("col"),
        P("col"),
        P("col"),
        P("col"),
        P("col"),
        P(("dp", "row"), "col"),
    )
    return jax.shard_map(
        local,
        mesh=mesh,
        in_specs=placed,
        out_specs=(
            P(("dp", "row"), "col"),
            P(("dp", "row"), "col"),
            P(("col", "dp"), "row"),
            P(("col", "dp"), "row"),
            P(("col", "dp"), "row"),
            P(("row", "dp")),
            P(("row", "dp")),
            P("row", ("col", "dp")),
            P(("col", "dp")),
            P(("col", "dp"), "row"),
            P(("row", "dp")),
            P("row", ("col", "dp")),
            P(("col", "dp")),
            P(("col", "dp")),
            P(("col", "dp")),
            P(("col", "dp")),
            P(("col", "dp")),
        ),
        check_vma=False,
    )
```

profile of v0, /device:TPU:0, one launch (start us, length us, event | category | flops | bytes accessed | tf_op | source)
XLA Modules:
  0.0 1200.8 jit_solution(18180007742090181113)
XLA Ops:
  17.7 25.9 %all-gather.9.cloned.1.call-done = bf16[3072,384]{1,0:T(8,128)(2,1)} async-done(((bf16[768,384]{1,0:T(8,128)(2,1)}), bf16[3072,384]{1,0:T(8,128)(2,1)}) %all-gather.9.cloned.1.call-update) | async-done | bytes 2359312 | tf_op jit(solution)/shard_map/all_gather | solution.py:34
  50.7 85.2 %reduce-scatter.23.cloned.1.call-done = f32[1536,576]{0,1:T(8,128)} async-done(((f32[3072,576]{0,1:T(8,128)}), f32[1536,576]{0,1:T(8,128)}) %reduce-scatter.23.cloned.1.call-update) | async-done | bytes 3538960 | tf_op jit(solution)/shard_map/reduce_scatter | solution.py:36
  139.1 40.6 %while.27 = (s32[]{:T(128)}, bf16[3,512,3,64]{1,3,2,0:T(8,128)(2,1)S(1)}, f32[3,3,512]{2,1,0:T(4,128)}, s32[3]{0:T(128)}, bf16[1536,3,64]{0,2,1:T(8,128)(2,1)S(1...) while((s32[]{:T(128)}, ...), condition=%wide.region_8.9_spmd, body=%wide.region_5.8_spmd.sunk | while | flops 633175040 | bytes 33089708 | solution.py:96
  181.2 22.9 %all-gather.11.cloned.1.call-done = bf16[3072,192]{0,1:T(8,128)(2,1)} async-done(((bf16[1536,192]{0,1:T(8,128)(2,1)}), bf16[3072,192]{0,1:T(8,128)(2,1)}) %all-gather.11.cloned.1.call-update) | async-done | bytes 1179664 | tf_op jit(solution)/shard_map/all_gather | solution.py:53
  209.2 47.3 %reduce-scatter.25.cloned.1.call-done = f32[768,384]{1,0:T(8,128)} async-done(((f32[3072,384]{1,0:T(8,128)}), f32[768,384]{1,0:T(8,128)}) %reduce-scatter.25.cloned.1.call-update) | async-done | bytes 1179664 | tf_op jit(solution)/shard_map/reduce_scatter | solution.py:55
  265.2 16.8 %all-gather.17.cloned.1.call-done = bf16[3072,384]{1,0:T(8,128)(2,1)} async-done(((bf16[768,384]{1,0:T(8,128)(2,1)}), bf16[3072,384]{1,0:T(8,128)(2,1)}) %all-gather.17.cloned.1.call-update) | async-done | bytes 2359312 | tf_op jit(solution)/shard_map/all_gather | solution.py:59
  282.0 7.9 fusion.63
  290.0 18.1 %all-gather.13.cloned.1.call-done = bf16[3072,384]{1,0:T(8,128)(2,1)} async-done(((bf16[768,384]{1,0:T(8,128)(2,1)}), bf16[3072,384]{1,0:T(8,128)(2,1)}) %all-gather.13.cloned.1.call-update) | async-done | bytes 2359312 | tf_op jit(solution)/shard_map/all_gather | solution.py:34
  308.1 7.9 fusion.61
  316.1 104.9 %reduce-scatter.31.cloned.1.call-done = f32[1536,768]{1,0:T(8,128)} async-done(((f32[3072,768]{1,0:T(8,128)}), f32[1536,768]{1,0:T(8,128)}) %reduce-scatter.31.cloned.1.call-update) | async-done | bytes 4718608 | tf_op jit(solution)/shard_map/reduce_scatter | solution.py:63
  421.0 112.9 %reduce-scatter.27.cloned.1.call-done = f32[1536,768]{1,0:T(8,128)} async-done(((f32[3072,768]{1,0:T(8,128)}), f32[1536,768]{1,0:T(8,128)}) %reduce-scatter.27.cloned.1.call-update) | async-done | bytes 4718608 | tf_op jit(solution)/shard_map/reduce_scatter | solution.py:36
  533.9 7.7 fusion.38
  542.3 62.2 %all-gather.19.cloned.1.call-done = bf16[3072,768]{1,0:T(8,128)(2,1)} async-done(((bf16[1536,768]{1,0:T(8,128)(2,1)}), bf16[3072,768]{1,0:T(8,128)(2,1)}) %all-gather.19.cloned.1.call-update) | async-done | bytes 4718608 | tf_op jit(solution)/shard_map/all_gather | solution.py:41
  604.5 7.1 fusion.64
  611.7 56.9 %all-gather.15.cloned.1.call-done = bf16[3072,768]{1,0:T(8,128)(2,1)} async-done(((bf16[1536,768]{1,0:T(8,128)(2,1)}), bf16[3072,768]{1,0:T(8,128)(2,1)}) %all-gather.15.cloned.1.call-update) | async-done | bytes 4718608 | tf_op jit(solution)/shard_map/all_gather | solution.py:53
  668.5 7.1 fusion.62
  675.9 43.0 %reduce-scatter.33.cloned.1.call-done = f32[768,384]{1,0:T(8,128)} async-done(((f32[3072,384]{1,0:T(8,128)}), f32[768,384]{1,0:T(8,128)}) %reduce-scatter.33.cloned.1.call-update) | async-done | bytes 1179664 | tf_op jit(solution)/shard_map/reduce_scatter | solution.py:48
  727.9 41.4 %reduce-scatter.29.cloned.1.call-done = f32[768,384]{1,0:T(8,128)} async-done(((f32[3072,384]{1,0:T(8,128)}), f32[768,384]{1,0:T(8,128)}) %reduce-scatter.29.cloned.1.call-update) | async-done | bytes 1179664 | tf_op jit(solution)/shard_map/reduce_scatter | solution.py:55
  772.7 24.2 %all-gather.21.cloned.1.call-done = bf16[3072,384]{1,0:T(8,128)(2,1)} async-done(((bf16[768,384]{1,0:T(8,128)(2,1)}), bf16[3072,384]{1,0:T(8,128)(2,1)}) %all-gather.21.cloned.1.call-update) | async-done | bytes 2359312 | tf_op jit(solution)/shard_map/all_gather | solution.py:59
  801.2 34.8 %reduce-scatter.35.cloned.1.call-done = f32[1536,192]{0,1:T(8,128)} async-done(((f32[3072,192]{0,1:T(8,128)}), f32[1536,192]{0,1:T(8,128)}) %reduce-scatter.35.cloned.1.call-update) | async-done | bytes 1179664 | tf_op jit(solution)/shard_map/reduce_scatter | solution.py:63
  838.1 101.9 %while.28 = (s32[]{:T(128)}, f32[1536,3,64]{0,2,1:T(8,128)S(1)}, f32[1536,3,64]{0,2,1:T(8,128)S(1)}, bf16[3,512,3,64]{1,3,2,0:T(8,128)(2,1)}, s32[3]{0:T(128)}, ...) while((s32[]{:T(128)}, f32[1536,3,64]{0,2,1:T(8,128)S(1)}, ...), condition=%wide.region_25.26_spmd.clone, body=%wide.region_23.25_spmd.clone.sunk | while | flops 1533541376 | bytes 139036976 | solution.py:142
  856.0 9.4 multiply_convert_fusion.3
  889.9 9.4 multiply_convert_fusion.3
  923.9 9.4 multiply_convert_fusion.3
  947.6 45.2 %all-gather.23.cloned.1.call-done = bf16[3072,576]{0,1:T(8,128)(2,1)} async-done(((bf16[1536,576]{0,1:T(8,128)(2,1)}), bf16[3072,576]{0,1:T(8,128)(2,1)}) %all-gather.23.cloned.1.call-update) | async-done | bytes 3538960 | tf_op jit(solution)/shard_map/all_gather | solution.py:41
  992.8 6.6 fusion.66
  1033.5 30.7 %reduce-scatter.37.cloned.1.call-done = f32[768,384]{1,0:T(8,128)} async-done(((f32[3072,384]{1,0:T(8,128)}), f32[768,384]{1,0:T(8,128)}) %reduce-scatter.37.cloned.1.call-update) | async-done | bytes 1179664 | tf_op jit(solution)/shard_map/reduce_scatter | solution.py:48
  1066.9 21.5 %all-reduce.10 = (f32[192]{0:T(256)}, f32[192]{0:T(256)}, f32[384]{0:T(512)}, f32[768]{0:T(1024)}, f32[384]{0:T(512)}, /*index=5*/f32[384]{0:T(512)}, f32[384]{0:T(512)}, f32[384]{0:T(512)}, f32[384]{0:T(512)}) all-reduce(f32[192]{0:T(256)} %get-tuple-element.281, ...), channel_id=13, replica_groups=mesh['dp'=4,'row'=4,'col'=2] {'dp'}, use_global_device_ids=true, to_apply=%region_35.36.clone | all-reduce | flops 3456 | bytes 27648
  1114.6 13.2 %reduce-scatter.41.cloned.1.call-done = f32[768,96]{0,1:T(8,128)} async-done(((f32[768,384]{0,1:T(8,128)}), f32[768,96]{0,1:T(8,128)}) %reduce-scatter.41.cloned.1.call-update) | async-done | bytes 294928 | tf_op jit(solution)/shard_map/reduce_scatter | solution.py:225
  1127.8 22.2 %reduce-scatter.47.cloned.1.call-done = f32[96,192]{1,0:T(8,128)} async-done(((f32[384,192]{1,0:T(8,128)}), f32[96,192]{1,0:T(8,128)}) %reduce-scatter.47.cloned.1.call-update) | async-done | bytes 73744
  1150.0 21.7 %reduce-scatter.45.cloned.1.call-done = f32[96,192]{1,0:T(8,128)} async-done(((f32[384,192]{1,0:T(8,128)}), f32[96,192]{1,0:T(8,128)}) %reduce-scatter.45.cloned.1.call-update) | async-done | bytes 73744
  1171.7 21.9 %reduce-scatter.43.cloned.1.call-done = f32[96,192]{1,0:T(8,128)} async-done(((f32[384,192]{1,0:T(8,128)}), f32[96,192]{1,0:T(8,128)}) %reduce-scatter.43.cloned.1.call-update) | async-done | bytes 73744
  (243 shorter events, 226.3 us)
Async XLA Ops:
  7.2 300.9 %copy-start = (bf16[384,768]{1,0:T(8,128)(2,1)S(1)}, bf16[384,768]{1,0:T(8,128)(2,1)}, u32[]{:S(2)}) copy-start(bf16[384,768]{1,0:T(8,128)(2,1)} %param.29) | copy-start | bytes 1769476
  7.2 36.3 %all-gather.9.cloned.1.call-start = ((), (), s32[]{:S(2)}) async-start(), calls=%async_computation.14 | async-start | bytes 2949120 | tf_op jit(solution)/shard_map/all_gather | solution.py:34
  17.5 118.4 %reduce-scatter.23.cloned.1.call-start = ((), (), s32[]{:S(2)}) async-start(), calls=%async_computation.15 | async-start | bytes 10616832 | tf_op jit(solution)/shard_map/reduce_scatter | solution.py:36
  50.1 87.1 %copy-start.34 = (f32[192]{0:T(256)S(1)}, f32[192]{0:T(256)}, u32[]{:S(2)}) copy-start(f32[192]{0:T(256)} %param.26) | copy-start | bytes 2308
  50.1 87.1 %copy-start.35 = (f32[192]{0:T(256)S(1)}, f32[192]{0:T(256)}, u32[]{:S(2)}) copy-start(f32[192]{0:T(256)} %param.25) | copy-start | bytes 2308
  50.1 153.9 %all-gather.11.cloned.1.call-start = ((), (), s32[]{:S(2)}) async-start(), calls=%async_computation.16 | async-start | bytes 1769472 | tf_op jit(solution)/shard_map/all_gather | solution.py:53
  181.1 75.4 %reduce-scatter.25.cloned.1.call-start = ((), (), s32[]{:S(2)}) async-start(), calls=%async_computation.17 | async-start | bytes 5898240 | tf_op jit(solution)/shard_map/reduce_scatter | solution.py:55
  208.5 54.6 %copy-start.31 = (f32[384]{0:T(512)S(1)}, f32[384]{0:T(512)}, u32[]{:S(2)}) copy-start(f32[384]{0:T(512)} %param.35) | copy-start | bytes 4612
  208.5 73.5 %all-gather.17.cloned.1.call-start = ((), (), s32[]{:S(2)}) async-start(), calls=%async_computation.22 | async-start | bytes 2949120 | tf_op jit(solution)/shard_map/all_gather | solution.py:59
  209.1 72.9 %copy-start.21 = (bf16[768,384]{1,0:T(8,128)(2,1)S(1)}, bf16[768,384]{1,0:T(8,128)(2,1)}, u32[]{:S(2)}) copy-start(bf16[768,384]{1,0:T(8,128)(2,1)} %param.31) | copy-start | bytes 1769476
  209.1 99.0 %all-gather.13.cloned.1.call-start = ((), (), s32[]{:S(2)}) async-start(), calls=%async_computation.18 | async-start | bytes 2949120 | tf_op jit(solution)/shard_map/all_gather | solution.py:34
  265.0 156.0 %reduce-scatter.31.cloned.1.call-start = ((), (), s32[]{:S(2)}) async-start(), calls=%async_computation.23 | async-start | bytes 14155776 | tf_op jit(solution)/shard_map/reduce_scatter | solution.py:63
  290.0 243.9 %reduce-scatter.27.cloned.1.call-start = ((), (), s32[]{:S(2)}) async-start(), calls=%async_computation.19 | async-start | bytes 14155776 | tf_op jit(solution)/shard_map/reduce_scatter | solution.py:36
  316.1 217.8 %copy-start.32 = (f32[768]{0:T(1024)S(1)}, f32[768]{0:T(1024)}, u32[]{:S(2)}) copy-start(f32[768]{0:T(1024)} %param.30) | copy-start | bytes 9220
  316.1 288.4 %all-gather.19.cloned.1.call-start = ((), (), s32[]{:S(2)}) async-start(), calls=%async_computation.24 | async-start | bytes 7077888 | tf_op jit(solution)/shard_map/all_gather | solution.py:41
  541.6 126.9 %all-gather.15.cloned.1.call-start = ((), (), s32[]{:S(2)}) async-start(), calls=%async_computation.20 | async-start | bytes 7077888 | tf_op jit(solution)/shard_map/all_gather | solution.py:53
  542.2 176.7 %reduce-scatter.33.cloned.1.call-start = ((), (), s32[]{:S(2)}) async-start(), calls=%async_computation.25 | async-start | bytes 5898240 | tf_op jit(solution)/shard_map/reduce_scatter | solution.py:48
  611.6 157.8 %reduce-scatter.29.cloned.1.call-start = ((), (), s32[]{:S(2)}) async-start(), calls=%async_computation.21 | async-start | bytes 5898240 | tf_op jit(solution)/shard_map/reduce_scatter | solution.py:55
  675.7 93.7 %copy-start.18 = (bf16[768,384]{1,0:T(8,128)(2,1)S(1)}, bf16[768,384]{1,0:T(8,128)(2,1)}, u32[]{:S(2)}) copy-start(bf16[768,384]{1,0:T(8,128)(2,1)} %param.37) | copy-start | bytes 1769476
  675.7 121.2 %all-gather.21.cloned.1.call-start = ((), (), s32[]{:S(2)}) async-start(), calls=%async_computation.26 | async-start | bytes 2949120 | tf_op jit(solution)/shard_map/all_gather | solution.py:59
  719.0 50.4 %copy-start.16 = (f32[768,384]{1,0:T(8,128)S(1)}, f32[768,384]{1,0:T(8,128)}, u32[]{:S(2)}) copy-start(f32[768,384]{1,0:T(8,128)} %reduce-scatter.33.cloned.1.call-done) | copy-start | bytes 3538948
  772.7 63.3 %reduce-scatter.35.cloned.1.call-start = ((), (), s32[]{:S(2)}) async-start(), calls=%async_computation.27 | async-start | bytes 3538944 | tf_op jit(solution)/shard_map/reduce_scatter | solution.py:63
  801.1 191.7 %all-gather.23.cloned.1.call-start = ((), (), s32[]{:S(2)}) async-start(), calls=%async_computation.28 | async-start | bytes 5308416 | tf_op jit(solution)/shard_map/all_gather | solution.py:41
  943.3 84.3 %reduce-scatter.49.cloned.1.call-start = ((), (), s32[]{:S(2)}) async-start(), calls=%async_computation.35 | async-start | bytes 491520
  947.3 116.9 %reduce-scatter.37.cloned.1.call-start = ((), (), s32[]{:S(2)}) async-start(), calls=%async_computation.29 | async-start | bytes 5898240 | tf_op jit(solution)/shard_map/reduce_scatter | solution.py:48
  999.5 115.1 %reduce-scatter.39.cloned.1.call-start = ((), (), s32[]{:S(2)}) async-start(), calls=%async_computation.30 | async-start | bytes 1474560 | tf_op jit(solution)/shard_map/reduce_scatter | solution.py:223
  1006.6 121.2 %reduce-scatter.41.cloned.1.call-start = ((), (), s32[]{:S(2)}) async-start(), calls=%async_computation.31 | async-start | bytes 1474560 | tf_op jit(solution)/shard_map/reduce_scatter | solution.py:225
  1013.0 137.0 %reduce-scatter.47.cloned.1.call-start = ((), (), s32[]{:S(2)}) async-start(), calls=%async_computation.34 | async-start | bytes 491520
  1018.1 153.6 %reduce-scatter.45.cloned.1.call-start = ((), (), s32[]{:S(2)}) async-start(), calls=%async_computation.33 | async-start | bytes 491520
  1026.6 167.0 %reduce-scatter.43.cloned.1.call-start = ((), (), s32[]{:S(2)}) async-start(), calls=%async_computation.32 | async-start | bytes 491520
  1030.2 82.2 %copy-start.15 = (f32[768,384]{1,0:T(8,128)S(1)}, f32[768,384]{1,0:T(8,128)}, u32[]{:S(2)}) copy-start(f32[768,384]{1,0:T(8,128)} %get-tuple-element.266) | copy-start | bytes 3538948
  1064.2 129.3 %copy-start.1 = (bf16[384,768]{1,0:T(8,128)(2,1)S(1)}, bf16[384,768]{1,0:T(8,128)(2,1)}, u32[]{:S(2)}) copy-start(bf16[384,768]{1,0:T(8,128)(2,1)} %param.29) | copy-start | bytes 1769476
  (33 other events, 574.1 us)
Sparse Core Ops, SparseCore 0:
  17.6 25.8 all-gather.8
  50.3 85.5 reduce-scatter.22
  181.2 22.7 all-gather.10
  208.7 47.8 reduce-scatter.24
  257.9 24.0 all-gather.16
  284.0 24.0 all-gather.12
  310.4 110.5 reduce-scatter.30
  423.3 110.5 reduce-scatter.26
  541.8 62.6 all-gather.18
  605.8 62.6 all-gather.14
  671.1 47.8 reduce-scatter.32
  721.5 47.7 reduce-scatter.28
  772.8 24.0 all-gather.20
  801.2 34.7 reduce-scatter.34
  943.4 49.3 all-gather.22
  995.1 20.5 reduce-scatter.48
  1018.1 46.0 reduce-scatter.36
  1067.0 29.8 reduce-scatter.38
  1099.9 27.8 reduce-scatter.40
  1130.6 19.3 reduce-scatter.46
  1152.8 18.8 reduce-scatter.44
  1174.6 18.8 reduce-scatter.42
where the time goes:
time: 1210 us; the launch traced here: 1200 us
  waiting for transfers between devices  853 us (70%)
  matrix products  139 us (11%)
  other arithmetic  86.7 us (7%)
  blocking collectives  50.2 us (4%)
  local copies, waits for them, and re-layouts  41.5 us (3%)
  between operations  17.2 us (1%)
    reduce_scatter x2, waiting for transfers between devices, project_up(): result = lax.psum_scatter(pieces, 'col', scatter_dimension=0, tiled=True)  198 us
    reduce_scatter x2, waiting for transfers between devices, down_back(): result = lax.psum_scatter(pieces, 'col', scatter_dimension=0, tiled=True)  140 us
    all_gather x2, waiting for transfers between devices, up_back(): gathered = lax.all_gather(grad_rows, 'col', axis=0, tiled=True)  107 us
    reduce_scatter x2, waiting for transfers between devices, project_down(): lax.psum_scatter(pieces, 'row', scatter_dimension=0, tiled=True)  88.8 us
    all_gather x2, waiting for transfers between devices, project_down(): gathered = lax.all_gather(values, 'col', axis=0, tiled=True)  79.8 us
    reduce_scatter x2, waiting for transfers between devices, up_back(): lax.psum_scatter(pieces, 'row', scatter_dimension=0, tiled=True)  73.7 us
    unnamed x26, waiting for transfers between devices  67.1 us
    all_gather x2, waiting for transfers between devices, project_up(): gathered = lax.all_gather(normed_rows, 'row', axis=0, tiled=True)  43.9 us
  transfers between devices with their start and end apart: 22, of which 20 were waited for; matrix products, arithmetic and copies ran while one was open for 8% of the time, Pallas kernels for 0%

commit v1 on v0

v1 whole, which is shorter than its diff:
```python
import functools
import jax
import jax.numpy as jnp
from jax import lax
from jax.experimental import pallas as pl
from jax.experimental.pallas import tpu as pltpu
from jax.sharding import PartitionSpec as P

HD = 64
QB = 256
EPS = 1e-05
bf16 = jnp.bfloat16
f32 = jnp.float32


def swap_y(value):
    return lax.ppermute(value, "row", [(r, r ^ 2) for r in range(lax.axis_size("row"))])


def swap_c(value):
    return lax.ppermute(value, "row", [(r, r ^ 1) for r in range(lax.axis_size("row"))])


def swap_x(value):
    return lax.ppermute(value, "col", [(i, i ^ 1) for i in range(lax.axis_size("col"))])


def dot(left, right):
    return jnp.dot(left, right, preferred_element_type=f32)


def dot_rt(left, right):
    return lax.dot_general(left, right, (((1,), (1,)), ((), ())), preferred_element_type=f32)


def dot_lt(left, right):
    return lax.dot_general(left, right, (((0,), (0,)), ((), ())), preferred_element_type=f32)


def causal(scores):
    rows = lax.broadcasted_iota(jnp.int32, scores.shape, 0)
    cols = lax.broadcasted_iota(jnp.int32, scores.shape, 1)
    return jnp.where(cols <= rows, scores, -1e30)


def split_heads(source, target, count, scaled):
    for i in range(count):
        part = source[:, HD * i : HD * (i + 1)]
        target[i] = part * jnp.asarray(HD**-0.5, part.dtype) if i < scaled else part


def forward_kernel(heads, qkv_ref, out_ref, log_ref, qkv, outs, logs):
    head = pl.program_id(0)

    @pl.when(head == 0)
    def _():
        split_heads(qkv_ref, qkv, 3 * heads, heads)

    length = qkv_ref.shape[0]
    for low in range(0, length, QB):
        high = low + QB
        query = qkv[head, low:high, :]
        last = causal(dot_rt(query, qkv[heads + head, low:high, :]))
        top = jnp.max(last, axis=1, keepdims=True)
        if low:
            first = dot_rt(query, qkv[heads + head, 0:low, :])
            top = jnp.maximum(top, jnp.max(first, axis=1, keepdims=True))
            first = jnp.exp(first - top)
        last = jnp.exp(last - top)
        total = jnp.sum(last, axis=1, keepdims=True)
        if low:
            total = total + jnp.sum(first, axis=1, keepdims=True)
        inverse = 1.0 / total
        out = dot((last * inverse).astype(bf16), qkv[2 * heads + head, low:high, :])
        if low:
            out = out + dot((first * inverse).astype(bf16), qkv[2 * heads + head, 0:low, :])
        outs[head, low:high, :] = out.astype(bf16)
        logs[head, low:high, :] = top + jnp.log(total)

    @pl.when(head == heads - 1)
    def _():
        out_ref[...] = jnp.concatenate([outs[i] for i in range(heads)], axis=1)
        log_ref[...] = jnp.concatenate([logs[i] for i in range(heads)], axis=1)


def backward_kernel(
    heads, qkv_ref, log_ref, up_ref, grad_ref, qkv, ups, logs, grads, key_sum, value_sum
):
    head = pl.program_id(0)

    @pl.when(head == 0)
    def _():
        split_heads(qkv_ref, qkv, 3 * heads, heads)
        split_heads(up_ref, ups, heads, 0)
        for i in range(heads):
            logs[i] = log_ref[:, i : i + 1]

    length = qkv_ref.shape[0]
    key_sum[...] = jnp.zeros_like(key_sum)
    value_sum[...] = jnp.zeros_like(value_sum)
    for low in range(0, length, QB):
        high = low + QB
        query = qkv[head, low:high, :]
        up = ups[head, low:high, :]
        log = logs[head, low:high, :]
        spans = [(low, high)] + ([(0, low)] if low else [])
        parts = []
        row_dot = 0.0
        for start, stop in spans:
            scores = dot_rt(query, qkv[heads + head, start:stop, :])
            if start == low:
                scores = causal(scores)
            probs = jnp.exp(scores - log)
            prob_grad = dot_rt(up, qkv[2 * heads + head, start:stop, :])
            row_dot = row_dot + jnp.sum(prob_grad * probs, axis=1, keepdims=True)
            value_sum[:, start:stop] += dot_lt(up, probs.astype(bf16))
            parts.append((probs, prob_grad))
        query_grad = 0.0
        for (start, stop), (probs, prob_grad) in zip(spans, parts):
            score_grad = (probs * (prob_grad - row_dot)).astype(bf16)
            query_grad = query_grad + dot(score_grad, qkv[heads + head, start:stop, :])
            key_sum[:, start:stop] += dot_lt(query, score_grad)
        grads[head, low:high, :] = (query_grad * HD**-0.5).astype(bf16)
    grads[heads + head] = key_sum[...].T.astype(bf16)
    grads[2 * heads + head] = value_sum[...].T.astype(bf16)

    @pl.when(head == heads - 1)
    def _():
        grad_ref[...] = jnp.concatenate([grads[i] for i in range(3 * heads)], axis=1)


def whole(shape):
    return pl.BlockSpec(shape, lambda head: (0,) * len(shape))


def attend(qkv):
    length, width = qkv.shape
    heads = width // (3 * HD)
    pairs = heads * length * (length + QB)
    return pl.pallas_call(
        functools.partial(forward_kernel, heads),
        grid=(heads,),
        in_specs=[whole((length, width))],
        out_specs=[whole((length, heads * HD)), whole((length, heads))],
        out_shape=[
            jax.ShapeDtypeStruct((length, heads * HD), bf16),
            jax.ShapeDtypeStruct((length, heads), f32),
        ],
        scratch_shapes=[
            pltpu.VMEM((3 * heads, length, HD), bf16),
            pltpu.VMEM((heads, length, HD), bf16),
            pltpu.VMEM((heads, length, 1), f32),
        ],
        compiler_params=pltpu.CompilerParams(vmem_limit_bytes=40 * 2**20),
        cost_estimate=pl.CostEstimate(
            flops=8 * pairs * HD, bytes_accessed=length * width * 4, transcendentals=pairs
        ),
    )(qkv)


def attend_back(qkv, log, up):
    length, width = qkv.shape
    heads = width // (3 * HD)
    pairs = heads * length * (length + QB)
    return pl.pallas_call(
        functools.partial(backward_kernel, heads),
        grid=(heads,),
        in_specs=[whole((length, width)), whole((length, heads)), whole((length, heads * HD))],
        out_specs=whole((length, width)),
        out_shape=jax.ShapeDtypeStruct((length, width), bf16),
        scratch_shapes=[
            pltpu.VMEM((3 * heads, length, HD), bf16),
            pltpu.VMEM((heads, length, HD), bf16),
            pltpu.VMEM((heads, length, 1), f32),
            pltpu.VMEM((3 * heads, length, HD), bf16),
            pltpu.VMEM((HD, length), f32),
            pltpu.VMEM((HD, length), f32),
        ],
        compiler_params=pltpu.CompilerParams(vmem_limit_bytes=48 * 2**20),
        cost_estimate=pl.CostEstimate(
            flops=20 * pairs * HD, bytes_accessed=length * width * 6, transcendentals=pairs
        ),
    )(qkv, log, up)


def layer_norm(values):
    center = jnp.mean(values, axis=1, keepdims=True)
    inverse = lax.rsqrt(jnp.mean(values * values, axis=1, keepdims=True) - center * center + EPS)
    return (values - center) * inverse, inverse


def gelu_tanh(values):
    return jax.nn.gelu(values, approximate=True)


def cat(parts, axis):
    return jnp.concatenate(parts, axis=axis)


def gather_blocks(block):
    half = block.shape[0] // 2
    beside = swap_x(block)
    above = swap_y(block)
    across = cat((swap_x(above[:half]), swap_y(beside[half:])), 0)
    return block, beside, above, across


def scatter_blocks(own, beside, above, across):
    half = own.shape[0] // 2
    for_above = swap_x(across[:half].astype(bf16)).astype(f32)
    for_beside = swap_y(across[half:].astype(bf16)).astype(f32)
    beside = cat((beside[:half], beside[half:] + for_beside), 0).astype(bf16)
    above = cat((above[:half] + for_above, above[half:]), 0).astype(bf16)
    return own + swap_x(beside).astype(f32) + swap_y(above).astype(f32)


def sum_dp(value):
    return lax.psum_scatter(value.astype(bf16), "dp", scatter_dimension=0, tiled=True).astype(f32)


def place(total, value, start):
    return lax.dynamic_update_slice_in_dim(total, value, start, 0)


def local(
    tokens,
    query_weight,
    key_weight,
    value_weight,
    query_bias,
    value_bias,
    out_weight,
    out_bias,
    up_weight,
    up_bias,
    down_weight,
    down_bias,
    attn_gain,
    attn_shift,
    mlp_gain,
    mlp_shift,
    cotangent,
):
    x = lax.axis_index("col")
    row = lax.axis_index("row")
    y, c = row // 2, row % 2
    z = lax.axis_index("dp")
    n_dp = lax.axis_size("dp")
    lined = x == y
    span, half = tokens.shape
    piece = span // 2
    width = 2 * half
    length = 2 * span
    part = query_weight.shape[1]
    hid = up_weight.shape[1]

    def pick(first, second):
        return jnp.where(lined, first, second), jnp.where(lined, second, first)

    other_tokens = swap_x(tokens)
    qkv_own = cat((query_weight, key_weight, value_weight), 1)
    qkv_other = swap_y(qkv_own)
    by_feature = jnp.stack((attn_gain, attn_shift, mlp_gain, mlp_shift, out_bias, down_bias))
    by_feature = cat((by_feature, swap_x(by_feature)), 1)
    by_unit = cat((query_bias, value_bias, up_bias), 0)
    by_unit_other = swap_y(by_unit)
    qkv_keep, qkv_send = pick(qkv_own, qkv_other)
    qkv_weight = cat((qkv_keep, swap_x(qkv_send)), 0)
    unit_keep, _ = pick(by_unit, by_unit_other)
    qkv_bias = cat((unit_keep[:part], jnp.zeros((part,), f32), unit_keep[part : 2 * part]), 0)
    up_bias_all = cat((by_unit[2 * part :], by_unit_other[2 * part :]), 0)
    first_gain, first_shift, second_gain, second_shift, out_b, down_b = by_feature

    cot_keep = lax.dynamic_slice_in_dim(cotangent, x * piece, piece, 0)
    cot_send = lax.dynamic_slice_in_dim(cotangent, (1 - x) * piece, piece, 0)
    cot_own = cat((cot_keep, swap_x(cot_send)), 1)
    cot_all = cat((cot_own, swap_c(cot_own)), 0)

    up_blocks = gather_blocks(cat((out_weight, up_weight[:, : hid // 2], up_weight[:, hid // 2 :]), 0))
    down_blocks = gather_blocks(down_weight)

    inputs = cat((tokens, other_tokens), 1).astype(f32)
    first_norm, first_inv = layer_norm(inputs)
    first_in = (first_norm * first_gain + first_shift).astype(bf16)
    first_all = place(jnp.zeros((length, width), bf16), first_in, c * span)
    first_all = place(first_all, swap_c(first_in), (1 - c) * span)
    qkv = (dot(first_all, qkv_weight) + qkv_bias).astype(bf16)
    attended, logsum = attend(qkv)

    def rows_of(value, col):
        return cat(
            [
                lax.dynamic_slice_in_dim(value, cc * span + col * piece, piece, 0)
                for cc in (c, 1 - c)
            ],
            0,
        )

    att_keep = rows_of(attended, x)
    att_got = swap_x(rows_of(attended, 1 - x))
    att_all = cat(pick(att_keep, att_got), 1)
    own, beside, above, across = (block[:part] for block in up_blocks)
    out_all = cat((cat((own, beside), 1), cat((above, across), 1)), 0)
    sums = dot(att_all, out_all)
    attn_out = sums[:piece] + swap_c(sums[piece:])
    mine = lax.dynamic_slice_in_dim(inputs, x * piece, piece, 0)
    middle = mine + (attn_out + out_b)
    second_norm, second_inv = layer_norm(middle)
    second_in = (second_norm * second_gain + second_shift).astype(bf16)
    second_all = cat((second_in, swap_c(second_in)), 0)

    own, beside, above, across = (
        cat((block[part : part + half], block[part + half :]), 1) for block in up_blocks
    )
    up_all = cat((cat((own, above), 1), cat((beside, across), 1)), 0)
    own, beside, above, across = down_blocks
    down_all = cat((cat((own, beside), 1), cat((above, across), 1)), 0)
    hidden_pre = dot(second_all, up_all) + up_bias_all
    hidden, gelu_back = jax.vjp(gelu_tanh, hidden_pre)
    hidden = hidden.astype(bf16)
    hidden_grad = dot_rt(cot_all, down_all)
    pre_grad = gelu_back(hidden_grad)[0].astype(bf16)
    sums = dot_rt(pre_grad, up_all)
    second_grad = sums[:piece] + swap_c(sums[piece:])
    scaled = second_grad * second_gain
    middle_grad = cot_own.astype(f32) + second_inv * (
        scaled
        - jnp.mean(scaled, axis=1, keepdims=True)
        - second_norm * jnp.mean(scaled * second_norm, axis=1, keepdims=True)
    )
    middle_low = middle_grad.astype(bf16)
    middle_all = cat((middle_low, swap_c(middle_low)), 0)
    att_grad = dot_rt(middle_all, out_all).astype(bf16)
    grad_keep, grad_send = pick(att_grad[:, :part], att_grad[:, part:])
    grad_got = swap_x(grad_send)
    up_att = jnp.zeros((length, part), bf16)
    for value, col in ((grad_keep, x), (grad_got, 1 - x)):
        up_att = place(up_att, value[:piece], c * span + col * piece)
        up_att = place(up_att, value[piece:], (1 - c) * span + col * piece)

    sums = dot(hidden, down_all)
    mlp_out = sums[:piece] + swap_c(sums[piece:])
    result = (middle + (mlp_out + down_b)).astype(bf16)
    outputs = place(jnp.zeros((span, half), bf16), result[:, :half], x * piece)
    outputs = place(outputs, swap_x(result[:, half:]), (1 - x) * piece)

    up_g = dot_lt(second_all, pre_grad)
    down_g = dot_lt(cot_all, hidden)
    out_g = dot_lt(middle_all, att_all)

    def block(first, second):
        rows = slice(first * half, (first + 1) * half)
        return cat(
            (
                up_g[rows, second * hid : (second + 1) * hid],
                down_g[rows, second * hid : (second + 1) * hid],
                out_g[rows, second * part : (second + 1) * part],
            ),
            1,
        )

    late = sum_dp(scatter_blocks(block(0, 0), block(1, 0), block(0, 1), block(1, 1)))
    up_w_grad = late[:, :hid]
    down_w_grad = late[:, hid : 2 * hid].T
    out_w_grad = late[:, 2 * hid :].T

    mid = place(jnp.zeros((span, half), f32), middle_grad[:, :half], x * piece)
    mid = place(mid, swap_x(middle_low[:, half:]).astype(f32), (1 - x) * piece)

    qkv_grad = attend_back(qkv, logsum, up_att)
    sums = dot_rt(qkv_grad, qkv_weight)
    sums = lax.dynamic_slice_in_dim(sums, c * span, span, 0) + swap_c(
        lax.dynamic_slice_in_dim(sums, (1 - c) * span, span, 0)
    )
    first_grad = sums[:, :half] + swap_x(sums[:, half:].astype(bf16)).astype(f32)
    own_norm = first_norm[:, :half]
    scaled = first_grad * attn_gain
    means = jnp.stack((jnp.sum(scaled, axis=1), jnp.sum(scaled * own_norm, axis=1)))
    means = (means + swap_x(means)) / width
    input_grad = mid + first_inv * (
        scaled - means[0][:, None] - own_norm * means[1][:, None]
    )

    qkv_g = dot_lt(first_all, qkv_grad)
    qkv_g_got = swap_x(qkv_g[half:].astype(bf16)).astype(f32)
    g_keep, g_send = pick(qkv_g[:half], qkv_g_got)
    qkv_w_grad = sum_dp(g_keep + swap_y(g_send.astype(bf16)).astype(f32))

    def at(vector, start, total):
        return lax.dynamic_update_slice(jnp.zeros((total,), f32), vector, (start,))

    def features(vector):
        return at(vector[:half], x * half, width) + at(vector[half:], (1 - x) * half, width)

    pre_sum = jnp.sum(pre_grad.astype(f32), axis=0)
    n_row = 2 * 2
    early = cat(
        (
            at(pre_sum[:hid], row * hid, n_row * hid)
            + at(pre_sum[hid:], (2 * (1 - y) + c) * hid, n_row * hid),
            features(jnp.sum(middle_low.astype(f32), axis=0)),
            at(jnp.sum(cotangent.astype(f32), axis=0), x * half, width),
            features(jnp.sum(second_grad * second_norm, axis=0)),
            features(jnp.sum(second_grad, axis=0)),
        ),
        0,
    )
    early = lax.psum(early, ("dp", "row", "col"))
    bias_sum = jnp.sum(qkv_grad.astype(f32), axis=0)
    group = (2 * x + c) * part
    final = cat(
        (
            at(bias_sum[:part], group, n_row * part),
            at(bias_sum[2 * part :], group, n_row * part),
            at(jnp.sum(first_grad * own_norm, axis=0), x * half, width),
            at(jnp.sum(first_grad, axis=0), x * half, width),
        ),
        0,
    )
    final = lax.psum(final, ("dp", "row", "col"))

    def take(vector, base, index, size):
        chunk = size // n_dp
        return lax.dynamic_slice(vector, (base + index * size + z * chunk,), (chunk,))

    base = n_row * hid
    return (
        outputs,
        input_grad,
        qkv_w_grad[:, :part],
        qkv_w_grad[:, part : 2 * part],
        qkv_w_grad[:, 2 * part :],
        take(final, 0, row, part),
        take(final, n_row * part, row, part),
        out_w_grad,
        take(early, base, x, half),
        up_w_grad,
        take(early, 0, row, hid),
        down_w_grad,
        take(early, base + width, x, half),
        take(final, 2 * n_row * part, x, half),
        take(final, 2 * n_row * part + width, x, half),
        take(early, base + 2 * width, x, half),
        take(early, base + 3 * width, x, half),
    )


def solution(mesh):
    placed = (
        P(("dp", "row"), "col"),
        P("col", "row"),
        P("col", "row"),
        P("col", "row"),
        P("row"),
        P("row"),
        P("row", "col"),
        P("col"),
        P("col", "row"),
        P("row"),
        P("row", "col"),
        P("col"),
        P("col"),
        P("col"),
        P("col"),
        P("col"),
        P(("dp", "row"), "col"),
    )
    return jax.shard_map(
        local,
        mesh=mesh,
        in_specs=placed,
        out_specs=(
            P(("dp", "row"), "col"),
            P(("dp", "row"), "col"),
            P(("col", "dp"), "row"),
            P(("col", "dp"), "row"),
            P(("col", "dp"), "row"),
            P(("row", "dp")),
            P(("row", "dp")),
            P("row", ("col", "dp")),
            P(("col", "dp")),
            P(("col", "dp"), "row"),
            P(("row", "dp")),
            P("row", ("col", "dp")),
            P(("col", "dp")),
            P(("col", "dp")),
            P(("col", "dp")),
            P(("col", "dp")),
            P(("col", "dp")),
        ),
        check_vma=False,
    )
```

time: 1210 us -> 391 us (0.32)
  waiting for transfers between devices: 853 us -> 91.1 us
  matrix products: 139 us -> 33.3 us
  local copies, waits for them, and re-layouts: 41.5 us -> 79.9 us
  Pallas kernels: 0 us -> 31 us
  starting transfers between devices: 1.54 us -> 31.2 us
  other arithmetic: 86.7 us -> 62.8 us
    reduce_scatter x10 -> x0, waiting for transfers between devices: 513 us -> none  [the longest x2 198 us: project_up(): result = lax.psum_scatter(pieces, 'col', scatter_dimension=0, tiled=True)]
    all_gather x8 -> x0, waiting for transfers between devices: 272 us -> none  [the longest x2 107 us: up_back(): gathered = lax.all_gather(grad_rows, 'col', axis=0, tiled=True)]
    dot_general x32 -> x12, matrix products: 136 us -> 33.3 us  [the longest x4 12.2 us: dot(): return jnp.dot(left, right, preferred_element_type=f32)]
    ppermute x0 -> x34, waiting for transfers between devices: none -> 87.8 us  [the longest x9 51.1 us: swap_y(): lax.ppermute(value, 'row', [(r, r ^ 2) for r in range(lax.axis_size('row'...]
    unnamed x26 -> x4, waiting for transfers between devices: 67.1 us -> 3.31 us
    convert_element_type x9 -> x5, other arithmetic: 47.1 us -> 6.88 us  [the longest x2 5.15 us: sum_dp(): value.astype(bf16)]
    ppermute x0 -> x34, starting transfers between devices: none -> 31.1 us  [the longest x17 21.9 us: swap_x(): lax.ppermute(value, 'col', [(i, i ^ 1) for i in range(lax.axis_size('col'...]
    pallas_call x0 -> x2, Pallas kernels: none -> 31 us  [the longest x1 17.4 us: attend_back(): pl.pallas_call(functools.partial(backward_kernel, heads), grid=(heads,),...]
  transfers between devices with their start and end apart: 22 -> 36, of which waited for: 20 -> 11; matrix products, arithmetic and copies ran while one was open for 8% -> 40% of each run, Pallas kernels for 0% -> 8%
where the time goes in v1:
time: 391 us; the launch traced here: 386 us
  waiting for transfers between devices  91.1 us (23%)
  local copies, waits for them, and re-layouts  79.9 us (20%)
  other arithmetic  62.8 us (16%)
  blocking collectives  41.2 us (11%)
  matrix products  33.3 us (9%)
  starting transfers between devices  31.2 us (8%)
  Pallas kernels  31 us (8%)
  between operations  15.3 us (4%)
    ppermute x9, waiting for transfers between devices, swap_y(): lax.ppermute(value, 'row', [(r, r ^ 2) for r in range(lax.axis_size('row'...  51.1 us
    psum x1, blocking collectives, local(): final = lax.psum(final, ('dp', 'row', 'col'))  41.2 us
    ppermute x17, waiting for transfers between devices, swap_x(): lax.ppermute(value, 'col', [(i, i ^ 1) for i in range(lax.axis_size('col'...  35.5 us
    unnamed x126, local copies, waits for them, and re-layouts  26.2 us
    concatenate x11, other arithmetic, cat(): return jnp.concatenate(parts, axis=axis)  25.8 us
    ppermute x17, starting transfers between devices, swap_x(): lax.ppermute(value, 'col', [(i, i ^ 1) for i in range(lax.axis_size('col'...  21.9 us
    pallas_call x1, Pallas kernels, attend_back(): pl.pallas_call(functools.partial(backward_kernel, heads), grid=(heads,),...  17.4 us
    pallas_call x1, Pallas kernels, attend(): pl.pallas_call(functools.partial(forward_kernel, heads), grid=(heads,), i...  13.5 us
  transfers between devices with their start and end apart: 36, of which 11 were waited for; matrix products, arithmetic and copies ran while one was open for 40% of the time, Pallas kernels for 8%

profile of v1, /device:TPU:0, one launch (start us, length us, event | category | flops | bytes accessed | tf_op | source)
XLA Modules:
  0.0 385.7 jit_solution(12002180443246622773)
XLA Ops:
  7.2 3.0 collective-permute-start
  20.2 3.9 %collective-permute-done.1 = f32[6,384]{1,0:T(8,128)S(1)} collective-permute-done((f32[6,384]{1,0:T(8,128)S(1)}, f32[6,384]{1,0:T(8,128)S(1)}, u32[]{:S(2)}, u32[]{:S(2)}) %collective-permute-start.1) | collective-permute-done | bytes 9248 | tf_op jit(solution)/shard_map/ppermute | solution.py:25
  27.2 2.7 constant_dynamic-update-slice_fusion.6
  35.0 15.0 %collective-permute-done.8 = bf16[960,384]{1,0:T(8,128)(2,1)S(1)} collective-permute-done((bf16[960,384]{1,0:T(8,128)(2,1)}, bf16[960,384]{1,0:T(8,128)(2,1)S(1)}, u32[]{:S(2)}, u32[]{:S(2)}) %collective-permute-start.8) | collective-permute-done | bytes 737312 | tf_op jit(solution)/shard_map/ppermute | solution.py:17
  52.6 2.4 constant_dynamic-update-slice_fusion.5
  55.0 6.7 %collective-permute-done.4 = bf16[384,576]{0,1:T(8,128)(2,1)S(1)} collective-permute-done((bf16[384,576]{0,1:T(8,128)(2,1)S(1)}, bf16[384,576]{0,1:T(8,128)(2,1)S(1)}, u32[]{:S(2)}, u32[]{:S(2)}) %collective-permute-start.4) | collective-permute-done | bytes 442400 | tf_op jit(solution)/shard_map/ppermute | solution.py:25
  61.7 3.9 %add_convert_fusion.qkv_ref = bf16[1536,576]{1,0:T(8,128)(2,1)S(1)} fusion(bf16[1536,768]{1,0:T(8,128)(2,1)} %constant_dynamic-update-slice_fusion.5, f32[576]{0:T(1024)S(1)} %pad_maximum_fusion.29, bf16[384,576]{0,1:T(8,128)(2,1)S(1)} %collective-permute-done.4, bf16[384,576]{0,1:T(8,128)(2,1)S(1)} %get-tuple-element.131), kind=kOutput, calls=%fused_computation.19 | convolution fusion | flops 1362493440 | bytes 5015808 | tf_op jit(solution)/shard_map/dot_general | solution.py:29
  65.6 13.5 %shard_map.296 = (bf16[1536,192]{1,0:T(8,128)(2,1)S(1)}, f32[1536,3]{1,0:T(8,128)S(1)}) custom-call(bf16[1536,576]{1,0:T(8,128)(2,1)S(1)} %add_convert_fusion.qkv_ref), custom_call_target="tpu_custom_call" | custom-call | flops 4227858432 | bytes 3538944 | tf_op jit(solution)/shard_map/pallas_call | solution.py:140
  88.5 4.6 %collective-permute-done.6 = bf16[768,192]{1,0:T(8,128)(2,1)} collective-permute-done((bf16[768,192]{1,0:T(8,128)(2,1)}, bf16[768,192]{1,0:T(8,128)(2,1)}, u32[]{:S(2)}, u32[]{:S(2)}) %collective-permute-start.6) | collective-permute-done | bytes 294944 | tf_op jit(solution)/shard_map/ppermute | solution.py:25
  99.4 10.4 %collective-permute-done.19 = bf16[384,384]{1,0:T(8,128)(2,1)} collective-permute-done((bf16[384,384]{1,0:T(8,128)(2,1)}, bf16[384,384]{1,0:T(8,128)(2,1)}, u32[]{:S(2)}, u32[]{:S(2)}) %collective-permute-start.19) | collective-permute-done | bytes 294944 | tf_op jit(solution)/shard_map/ppermute | solution.py:25
  120.8 8.4 %collective-permute-done.12 = bf16[480,384]{1,0:T(8,128)(2,1)S(1)} collective-permute-done((bf16[480,384]{1,0:T(8,128)(2,1)S(1)}, bf16[480,384]{1,0:T(8,128)(2,1)S(1)}, u32[]{:S(2)}, u32[]{:S(2)}) %collective-permute-start.12) | collective-permute-done | bytes 368672 | tf_op jit(solution)/shard_map/ppermute | solution.py:17
  131.3 18.1 %fusion.16 = bf16[768,1536]{1,0:T(8,128)(2,1)S(1)} fusion(bf16[480,384]{1,0:T(8,128)(2,1)S(1)} %collective-permute-done.12, bf16[480,384]{1,0:T(8,128)(2,1)} %collective-permute-done.9, bf16[384,384]{1,0:T(8,128)(2,1)S(1)} %slice.320, bf16[384,384]{1,0:T(8,128)(2,1)S(1)} %get-tuple-element.142, bf16[384,384]{1,0:T(8,128)(2,1)S(1)} %get-tuple-element.141, ...), kind=kLoop, calls=%fused_computation.29 | loop fusion | flops 27131904 | bytes 5160960 | tf_op jit(solution)/shard_map/concatenate | solution.py:197
  151.5 6.2 %convert_reduce_fusion = (f32[1536]{0:T(1024)S(1)}, bf16[768,1536]{1,0:T(8,128)(2,1)S(1)}) fusion(f32[768,1536]{1,0:T(8,128)S(1)} %fusion.29, f32[1536]{0:T(1024)S(1)} %pad_maximum_fusion.27, bf16[384,384]{1,0:T(8,128)(2,1)S(1)} %collective-permute-done.16, bf16[384,384]{1,0:T(8,128)(2,1)S(1)} %collective-permute-done.15, ...), kind=kOutput, calls=%fused_computation.14 | convolution fusion | flops 1854405120 | bytes 10629120 | tf_op jit(solution)/shard_map/dot_general | solution.py:33
  162.1 4.4 %fusion.46 = f32[768,768]{1,0:T(8,128)S(1)} fusion(bf16[384,384]{1,0:T(8,128)(2,1)S(1)} %collective-permute-done.16, bf16[384,384]{1,0:T(8,128)(2,1)S(1)} %collective-permute-done.15, bf16[768,384]{1,0:T(8,128)(2,1)} %collective-permute-done.14, bf16[768,384]{1,0:T(8,128)(2,1)} %collective-permute-done.13, bf16[768,384]{1,0:T(8,128)(2,1)} %param.27, ...), kind=kOutput, calls=%fused_computation.167 | convolution fusion | flops 1835532288 | bytes 9443328 | tf_op jit(solution)/shard_map/dot_general | solution.py:29
  168.3 3.2 fusion.31
  171.6 2.5 fusion.28
  180.9 2.7 copy.92
  183.9 2.4 multiply_reduce_fusion.1
  186.3 3.1 convert_reduce_fusion.4
  216.9 17.4 %shard_map.297 = bf16[1536,576]{1,0:T(8,128)(2,1)S(1)} custom-call(bf16[1536,576]{1,0:T(8,128)(2,1)S(1)} %copy-done.1, f32[1536,3]{1,0:T(8,128)S(1)} %get-tuple-element.20.log_ref, bf16[1536,192]{1,0:T(8,128)(2,1)S(1)} %slice_dynamic-update-slice_fusion.2.up_ref), custom_call_target="tpu_custom_call" | custom-call | flops 10569646080 | bytes 5308416 | tf_op jit(solution)/shard_map/pallas_call | solution.py:165
  239.2 3.4 fusion.64
  246.8 2.5 copy.80
  253.4 2.8 copy.78
  262.5 27.6 %collective-permute-done.29 = bf16[384,576]{0,1:T(8,128)(2,1)S(1)} collective-permute-done((bf16[384,576]{0,1:T(8,128)(2,1)S(1)}, bf16[384,576]{0,1:T(8,128)(2,1)S(1)}, u32[]{:S(2)}, u32[]{:S(2)}) %collective-permute-start.29) | collective-permute-done | bytes 442400 | tf_op jit(solution)/shard_map/ppermute | solution.py:17
  294.6 4.0 %collective-permute-done.22 = bf16[384,384]{1,0:T(8,128)(2,1)} collective-permute-done((bf16[384,384]{1,0:T(8,128)(2,1)}, bf16[384,384]{1,0:T(8,128)(2,1)}, u32[]{:S(2)}, u32[]{:S(2)}) %collective-permute-start.22) | collective-permute-done | bytes 294944 | tf_op jit(solution)/shard_map/ppermute | solution.py:25
  300.4 4.0 %fusion.12 = bf16[384,1728]{0,1:T(8,128)(2,1)} fusion(f32[384,192]{0,1:T(8,128)S(1)} %copy-done.29, f32[384,768]{0,1:T(8,128)} %copy.93, f32[384,768]{0,1:T(8,128)} %copy.92, bf16[384,1728]{0,1:T(8,128)(2,1)} %collective-permute-done.33, bf16[384,1728]{0,1:T(8,128)(2,1)} %collective-permute-done.31), kind=kLoop, calls=%fused_computation.25 | loop fusion | flops 4644864 | bytes 6635520 | tf_op jit(solution)/shard_map/convert_element_type | solution.py:218
  304.4 2.5 copy.90
  307.4 2.7 dynamic-slice_add_fusion
  312.3 3.3 reduce-scatter.7.cloned.1.call-done
  318.9 5.9 %collective-permute-done.26 = bf16[768,384]{1,0:T(8,128)(2,1)S(1)} collective-permute-done((bf16[768,384]{1,0:T(8,128)(2,1)}, bf16[768,384]{1,0:T(8,128)(2,1)S(1)}, u32[]{:S(2)}, u32[]{:S(2)}) %collective-permute-start.26) | collective-permute-done | bytes 589856 | tf_op jit(solution)/shard_map/ppermute | solution.py:25
  328.2 41.2 %all-reduce = (f32[3072]{0:T(1024)S(1)}, f32[6144]{0:T(1024)S(1)}) all-reduce(f32[3072]{0:T(1024)S(1)} %pad_maximum_fusion.26, f32[6144]{0:T(1024)S(1)} %constant_dynamic-update-slice_fusion.7), channel_id=1, replica_groups=mesh['dp'=4,'row'=4,'col'=2] {'dp','row','col'}, use_global_device_ids=true, to_apply=%region_12.13 | all-reduce | flops 9216 | bytes 73728 | tf_op jit(solution)/shard_map/psum | solution.py:420
  371.8 3.0 multiply_add_fusion
  (312 shorter events, 132.9 us)
Async XLA Ops:
  7.2 308.4 %reduce-scatter.7.cloned.1.call-start = ((), (), s32[]{:S(2)}) async-start(), calls=%async_computation.2 | async-start | bytes 614400
  7.2 16.9 %collective-permute-start = (bf16[768,384]{1,0:T(8,128)(2,1)}, bf16[768,384]{1,0:T(8,128)(2,1)S(1)}, u32[]{:S(2)}, u32[]{:S(2)}) collective-permute-start(bf16[768,384]{1,0:T(8,128)(2,1)} %param.17), channel_id=1, source_target_pairs={{0,1},{1,0},{2,3},{3,2},{4,5},{5,4},{6,7},{7,6},{8,9},{9,8},{10,11... | collective-permute-start | bytes 1769480 | tf_op jit(solution)/shard_map/ppermute | solution.py:25
  15.3 18.9 %collective-permute-start.5 = (f32[1152]{0:T(1024)S(1)}, f32[1152]{0:T(1024)S(1)}, u32[]{:S(2)}, u32[]{:S(2)}) collective-permute-start(f32[1152]{0:T(1024)S(1)} %concatenate.109), channel_id=1, source_target_pairs={{0,4},{2,6},{4,0},{6,2},{1,5},{3,7},{5,1},{7,3},{8,12},{10,14},{12... | collective-permute-start | bytes 13832 | tf_op jit(solution)/shard_map/ppermute | solution.py:17
  20.1 14.1 %collective-permute-start.3 = (bf16[384,576]{0,1:T(8,128)(2,1)S(1)}, bf16[384,576]{0,1:T(8,128)(2,1)S(1)}, u32[]{:S(2)}, u32[]{:S(2)}) collective-permute-start(bf16[384,576]{0,1:T(8,128)(2,1)S(1)} %constant_dynamic-update-slice_fusion), channel_id=1, source_target_pairs={{0,4},{2,6},{4,0},{6,2},{1,5},{3,7},{5,1},{7,3},{8,12},{10,14},{12... | collective-permute-start | bytes 1327112 | tf_op jit(solution)/shard_map/ppermute | solution.py:17
  29.9 22.7 %collective-permute-start.2 = (bf16[768,768]{1,0:T(8,128)(2,1)}, bf16[768,768]{1,0:T(8,128)(2,1)}, u32[]{:S(2)}, u32[]{:S(2)}) collective-permute-start(bf16[768,768]{1,0:T(8,128)(2,1)} %get-tuple-element.117), channel_id=1, source_target_pairs={{0,2},{2,0},{4,6},{6,4},{1,3},{3,1},{5,7},{7,5},{8,10},{10,8},{12,... | collective-permute-start | bytes 3538952 | tf_op jit(solution)/shard_map/ppermute | solution.py:21
  30.9 19.1 %collective-permute-start.8 = (bf16[960,384]{1,0:T(8,128)(2,1)}, bf16[960,384]{1,0:T(8,128)(2,1)S(1)}, u32[]{:S(2)}, u32[]{:S(2)}) collective-permute-start(bf16[960,384]{1,0:T(8,128)(2,1)} %pad_maximum_fusion.13), channel_id=1, source_target_pairs={{0,4},{2,6},{4,0},{6,2},{1,5},{3,7},{5,1},{7,3},{8,12},{10,14},{12... | collective-permute-start | bytes 2211848 | tf_op jit(solution)/shard_map/ppermute | solution.py:17
  32.7 52.1 %collective-permute-start.7 = (bf16[960,384]{1,0:T(8,128)(2,1)}, bf16[960,384]{1,0:T(8,128)(2,1)}, u32[]{:S(2)}, u32[]{:S(2)}) collective-permute-start(bf16[960,384]{1,0:T(8,128)(2,1)} %pad_maximum_fusion.13), channel_id=1, source_target_pairs={{0,1},{1,0},{2,3},{3,2},{4,5},{5,4},{6,7},{7,6},{8,9},{9,8},{10,11... | collective-permute-start | bytes 2211848 | tf_op jit(solution)/shard_map/ppermute | solution.py:25
  34.3 27.4 %collective-permute-start.4 = (bf16[384,576]{0,1:T(8,128)(2,1)S(1)}, bf16[384,576]{0,1:T(8,128)(2,1)S(1)}, u32[]{:S(2)}, u32[]{:S(2)}) collective-permute-start(bf16[384,576]{0,1:T(8,128)(2,1)S(1)} %get-tuple-element.132), channel_id=1, source_target_pairs={{0,1},{1,0},{2,3},{3,2},{4,5},{5,4},{6,7},{7,6},{8,9},{9,8},{10,11... | collective-permute-start | bytes 1327112 | tf_op jit(solution)/shard_map/ppermute | solution.py:25
  50.9 36.7 %collective-permute-start.9 = (bf16[480,384]{1,0:T(8,128)(2,1)}, bf16[480,384]{1,0:T(8,128)(2,1)}, u32[]{:S(2)}, u32[]{:S(2)}) collective-permute-start(bf16[480,384]{1,0:T(8,128)(2,1)} %slice.311), channel_id=1, source_target_pairs={{0,1},{1,0},{2,3},{3,2},{4,5},{5,4},{6,7},{7,6},{8,9},{9,8},{10,11... | collective-permute-start | bytes 1105928 | tf_op jit(solution)/shard_map/ppermute | solution.py:25
  80.8 12.4 %collective-permute-start.6 = (bf16[768,192]{1,0:T(8,128)(2,1)}, bf16[768,192]{1,0:T(8,128)(2,1)}, u32[]{:S(2)}, u32[]{:S(2)}) collective-permute-start(bf16[768,192]{1,0:T(8,128)(2,1)} %pad_maximum_fusion.23), channel_id=1, source_target_pairs={{0,1},{1,0},{2,3},{3,2},{4,5},{5,4},{6,7},{7,6},{8,9},{9,8},{10,11... | collective-permute-start | bytes 884744 | tf_op jit(solution)/shard_map/ppermute | solution.py:25
  82.3 28.6 %collective-permute-start.13 = (bf16[768,384]{1,0:T(8,128)(2,1)}, bf16[768,384]{1,0:T(8,128)(2,1)}, u32[]{:S(2)}, u32[]{:S(2)}) collective-permute-start(bf16[768,384]{1,0:T(8,128)(2,1)} %param.27), channel_id=1, source_target_pairs={{0,1},{1,0},{2,3},{3,2},{4,5},{5,4},{6,7},{7,6},{8,9},{9,8},{10,11... | collective-permute-start | bytes 1769480 | tf_op jit(solution)/shard_map/ppermute | solution.py:25
  82.8 29.5 %collective-permute-start.14 = (bf16[768,384]{1,0:T(8,128)(2,1)}, bf16[768,384]{1,0:T(8,128)(2,1)}, u32[]{:S(2)}, u32[]{:S(2)}) collective-permute-start(bf16[768,384]{1,0:T(8,128)(2,1)} %param.27), channel_id=1, source_target_pairs={{0,4},{2,6},{4,0},{6,2},{1,5},{3,7},{5,1},{7,3},{8,12},{10,14},{12... | collective-permute-start | bytes 1769480 | tf_op jit(solution)/shard_map/ppermute | solution.py:17
  84.8 25.0 %collective-permute-start.19 = (bf16[384,384]{1,0:T(8,128)(2,1)}, bf16[384,384]{1,0:T(8,128)(2,1)}, u32[]{:S(2)}, u32[]{:S(2)}) collective-permute-start(bf16[384,384]{1,0:T(8,128)(2,1)} %get-tuple-element.146), channel_id=1, source_target_pairs={{0,1},{1,0},{2,3},{3,2},{4,5},{5,4},{6,7},{7,6},{8,9},{9,8},{10,11... | collective-permute-start | bytes 884744 | tf_op jit(solution)/shard_map/ppermute | solution.py:25
  98.9 30.3 %collective-permute-start.10 = (f32[384,768]{1,0:T(8,128)}, f32[384,768]{1,0:T(8,128)}, u32[]{:S(2)}, u32[]{:S(2)}) collective-permute-start(f32[384,768]{1,0:T(8,128)} %slice.314), channel_id=1, source_target_pairs={{0,2},{2,0},{4,6},{6,4},{1,3},{3,1},{5,7},{7,5},{8,10},{10,8},{12,... | collective-permute-start | bytes 3538952 | tf_op jit(solution)/shard_map/ppermute | solution.py:21
  110.8 40.7 %collective-permute-start.20 = (bf16[384,768]{1,0:T(8,128)(2,1)S(1)}, bf16[384,768]{1,0:T(8,128)(2,1)S(1)}, u32[]{:S(2)}, u32[]{:S(2)}) collective-permute-start(bf16[384,768]{1,0:T(8,128)(2,1)S(1)} %pad_maximum_fusion.15), channel_id=1, source_target_pairs={{0,2},{2,0},{4,6},{6,4},{1,3},{3,1},{5,7},{7,5},{8,10},{10,8},{12,... | collective-permute-start | bytes 1769480 | tf_op jit(solution)/shard_map/ppermute | solution.py:21
  111.9 39.6 %collective-permute-start.16 = (bf16[384,384]{1,0:T(8,128)(2,1)S(1)}, bf16[384,384]{1,0:T(8,128)(2,1)S(1)}, u32[]{:S(2)}, u32[]{:S(2)}) collective-permute-start(bf16[384,384]{1,0:T(8,128)(2,1)S(1)} %slice.323), channel_id=1, source_target_pairs={{0,4},{2,6},{4,0},{6,2},{1,5},{3,7},{5,1},{7,3},{8,12},{10,14},{12... | collective-permute-start | bytes 884744 | tf_op jit(solution)/shard_map/ppermute | solution.py:17
  113.3 38.2 %collective-permute-start.15 = (bf16[384,384]{1,0:T(8,128)(2,1)S(1)}, bf16[384,384]{1,0:T(8,128)(2,1)S(1)}, u32[]{:S(2)}, u32[]{:S(2)}) collective-permute-start(bf16[384,384]{1,0:T(8,128)(2,1)S(1)} %slice.322), channel_id=1, source_target_pairs={{0,1},{1,0},{2,3},{3,2},{4,5},{5,4},{6,7},{7,6},{8,9},{9,8},{10,11... | collective-permute-start | bytes 884744 | tf_op jit(solution)/shard_map/ppermute | solution.py:25
  131.3 18.2 %collective-permute-start.11 = (bf16[384,768]{1,0:T(8,128)(2,1)S(1)}, bf16[384,768]{1,0:T(8,128)(2,1)S(1)}, u32[]{:S(2)}, u32[]{:S(2)}) collective-permute-start(bf16[384,768]{1,0:T(8,128)(2,1)S(1)} %add_convert_fusion.2), channel_id=1, source_target_pairs={{0,2},{2,0},{4,6},{6,4},{1,3},{3,1},{5,7},{7,5},{8,10},{10,8},{12,... | collective-permute-start | bytes 1769480 | tf_op jit(solution)/shard_map/ppermute | solution.py:21
  161.6 22.3 %collective-permute-start.21 = (f32[384,768]{1,0:T(8,128)}, f32[384,768]{1,0:T(8,128)}, u32[]{:S(2)}, u32[]{:S(2)}) collective-permute-start(f32[384,768]{1,0:T(8,128)} %slice.329), channel_id=1, source_target_pairs={{0,2},{2,0},{4,6},{6,4},{1,3},{3,1},{5,7},{7,5},{8,10},{10,8},{12,... | collective-permute-start | bytes 3538952 | tf_op jit(solution)/shard_map/ppermute | solution.py:21
  168.3 18.0 %collective-permute-start.17 = (f32[384,768]{1,0:T(8,128)}, f32[384,768]{1,0:T(8,128)}, u32[]{:S(2)}, u32[]{:S(2)}) collective-permute-start(f32[384,768]{1,0:T(8,128)} %slice.325), channel_id=1, source_target_pairs={{0,2},{2,0},{4,6},{6,4},{1,3},{3,1},{5,7},{7,5},{8,10},{10,8},{12,... | collective-permute-start | bytes 3538952 | tf_op jit(solution)/shard_map/ppermute | solution.py:21
  190.3 103.3 %collective-permute-start.18 = (bf16[384,384]{1,0:T(8,128)(2,1)}, bf16[384,384]{1,0:T(8,128)(2,1)}, u32[]{:S(2)}, u32[]{:S(2)}) collective-permute-start(bf16[384,384]{1,0:T(8,128)(2,1)} %get-tuple-element.147), channel_id=1, source_target_pairs={{0,1},{1,0},{2,3},{3,2},{4,5},{5,4},{6,7},{7,6},{8,9},{9,8},{10,11... | collective-permute-start | bytes 884744 | tf_op jit(solution)/shard_map/ppermute | solution.py:25
  198.0 16.9 %collective-permute-start.24 = (bf16[768,192]{1,0:T(8,128)(2,1)}, bf16[768,192]{1,0:T(8,128)(2,1)}, u32[]{:S(2)}, u32[]{:S(2)}) collective-permute-start(bf16[768,192]{1,0:T(8,128)(2,1)} %get-tuple-element.143), channel_id=1, source_target_pairs={{0,1},{1,0},{2,3},{3,2},{4,5},{5,4},{6,7},{7,6},{8,9},{9,8},{10,11... | collective-permute-start | bytes 884744 | tf_op jit(solution)/shard_map/ppermute | solution.py:25
  207.7 36.6 %collective-permute-start.32 = (bf16[192,1728]{1,0:T(8,128)(2,1)}, bf16[192,1728]{1,0:T(8,128)(2,1)}, u32[]{:S(2)}, u32[]{:S(2)}) collective-permute-start(bf16[192,1728]{1,0:T(8,128)(2,1)} %get-tuple-element.125), channel_id=1, source_target_pairs={{0,1},{1,0},{2,3},{3,2},{4,5},{5,4},{6,7},{7,6},{8,9},{9,8},{10,11... | collective-permute-start | bytes 1990664 | tf_op jit(solution)/shard_map/ppermute | solution.py:25
  211.1 39.5 %collective-permute-start.30 = (bf16[192,1728]{1,0:T(8,128)(2,1)}, bf16[192,1728]{1,0:T(8,128)(2,1)}, u32[]{:S(2)}, u32[]{:S(2)}) collective-permute-start(bf16[192,1728]{1,0:T(8,128)(2,1)} %get-tuple-element.124), channel_id=1, source_target_pairs={{0,4},{2,6},{4,0},{6,2},{1,5},{3,7},{5,1},{7,3},{8,12},{10,14},{12... | collective-permute-start | bytes 1990664 | tf_op jit(solution)/shard_map/ppermute | solution.py:17
  239.2 68.2 %collective-permute-start.25 = (f32[768,768]{1,0:T(8,128)}, f32[768,768]{1,0:T(8,128)}, u32[]{:S(2)}, u32[]{:S(2)}) collective-permute-start(f32[768,768]{1,0:T(8,128)} %constant_dynamic-slice_fusion), channel_id=1, source_target_pairs={{0,2},{2,0},{4,6},{6,4},{1,3},{3,1},{5,7},{7,5},{8,10},{10,8},{12,... | collective-permute-start | bytes 7077896 | tf_op jit(solution)/shard_map/ppermute | solution.py:21
  243.5 14.3 %collective-permute-start.28 = (bf16[384,576]{0,1:T(8,128)(2,1)}, bf16[384,576]{0,1:T(8,128)(2,1)S(1)}, u32[]{:S(2)}, u32[]{:S(2)}) collective-permute-start(bf16[384,576]{0,1:T(8,128)(2,1)} %slice.439), channel_id=1, source_target_pairs={{0,1},{1,0},{2,3},{3,2},{4,5},{5,4},{6,7},{7,6},{8,9},{9,8},{10,11... | collective-permute-start | bytes 1327112 | tf_op jit(solution)/shard_map/ppermute | solution.py:25
  249.3 51.1 %collective-permute-start.33 = (bf16[384,1728]{0,1:T(8,128)(2,1)}, bf16[384,1728]{0,1:T(8,128)(2,1)}, u32[]{:S(2)}, u32[]{:S(2)}) collective-permute-start(bf16[384,1728]{0,1:T(8,128)(2,1)} %copy.80), channel_id=1, source_target_pairs={{0,4},{2,6},{4,0},{6,2},{1,5},{3,7},{5,1},{7,3},{8,12},{10,14},{12... | collective-permute-start | bytes 3981320 | tf_op jit(solution)/shard_map/ppermute | solution.py:17
  256.3 44.1 %collective-permute-start.31 = (bf16[384,1728]{0,1:T(8,128)(2,1)}, bf16[384,1728]{0,1:T(8,128)(2,1)}, u32[]{:S(2)}, u32[]{:S(2)}) collective-permute-start(bf16[384,1728]{0,1:T(8,128)(2,1)} %copy.78), channel_id=1, source_target_pairs={{0,1},{1,0},{2,3},{3,2},{4,5},{5,4},{6,7},{7,6},{8,9},{9,8},{10,11... | collective-permute-start | bytes 3981320 | tf_op jit(solution)/shard_map/ppermute | solution.py:25
  259.2 30.9 %collective-permute-start.29 = (bf16[384,576]{0,1:T(8,128)(2,1)S(1)}, bf16[384,576]{0,1:T(8,128)(2,1)S(1)}, u32[]{:S(2)}, u32[]{:S(2)}) collective-permute-start(bf16[384,576]{0,1:T(8,128)(2,1)S(1)} %fusion.26), channel_id=1, source_target_pairs={{0,4},{2,6},{4,0},{6,2},{1,5},{3,7},{5,1},{7,3},{8,12},{10,14},{12... | collective-permute-start | bytes 1327112 | tf_op jit(solution)/shard_map/ppermute | solution.py:17
  293.5 81.3 %reduce-scatter.9.cloned.1.call-start = ((), (), s32[]{:S(2)}) async-start(), calls=%async_computation.3 | async-start | bytes 1720320
  311.0 13.8 %collective-permute-start.26 = (bf16[768,384]{1,0:T(8,128)(2,1)}, bf16[768,384]{1,0:T(8,128)(2,1)S(1)}, u32[]{:S(2)}, u32[]{:S(2)}) collective-permute-start(bf16[768,384]{1,0:T(8,128)(2,1)} %slice.438), channel_id=1, source_target_pairs={{0,1},{1,0},{2,3},{3,2},{4,5},{5,4},{6,7},{7,6},{8,9},{9,8},{10,11... | collective-permute-start | bytes 1769480 | tf_op jit(solution)/shard_map/ppermute | solution.py:25
  326.6 45.2 %collective-permute-start.27 = (f32[2,768]{1,0:T(2,128)S(1)}, f32[2,768]{1,0:T(2,128)S(1)}, u32[]{:S(2)}, u32[]{:S(2)}) collective-permute-start(f32[2,768]{1,0:T(2,128)S(1)} %pad_maximum_fusion.28), channel_id=1, source_target_pairs={{0,1},{1,0},{2,3},{3,2},{4,5},{5,4},{6,7},{7,6},{8,9},{9,8},{10,11... | collective-permute-start | bytes 18440 | tf_op jit(solution)/shard_map/ppermute | solution.py:25
  (57 other events, 523.1 us)
Sparse Core Ops, SparseCore 0:
  293.6 21.9 reduce-scatter.6
  318.0 30.5 reduce-scatter.8
